TPU v7x, 256 devices: a whole 4x4x8 slice. The times are simulated.
256 devices in a mesh: dp: 128 (over x_lo, z, y, core), rows: 2 (over x_hi).
Axes of the slice: x: 4 (x_hi: 2, x_lo: 2; x = x_hi * 2 + x_lo), y: 4, z: 8, core: 2. Of those that a mesh axis runs over, the one named last changes fastest.
Arguments:
- latents: bfloat16 [128, 4, 128, 320], P('dp', 'rows'), may hold values from -6 to 6
- mean_one: float32 [128, 32], P('dp'), may hold values from -0.5 to 0.5
- rstd_one: float32 [128, 32], P('dp'), may hold values from 0.5 to 2
- gain_one: float32 [320], replicated, may hold values from 0.25 to 1.75
- shift_one: float32 [320], replicated, may hold values from -0.5 to 0.5
- kernel_one: bfloat16 [4, 9, 25600], P(None, None, 'dp'), may hold values from -0.109375 to 0.109375
- bias_one: float32 [320], replicated, may hold values from -3 to 3
- embed_bias: float32 [128, 320], P('dp'), may hold values from -3 to 3
- mean_two: float32 [128, 32], P('dp'), may hold values from -0.5 to 0.5
- rstd_two: float32 [128, 32], P('dp'), may hold values from 0.5 to 2
- gain_two: float32 [320], replicated, may hold values from 0.25 to 1.75
- shift_two: float32 [320], replicated, may hold values from -0.5 to 0.5
- kernel_two: bfloat16 [4, 9, 25600], P(None, None, 'dp'), may hold values from -0.109375 to 0.109375
- bias_two: float32 [320], replicated, may hold values from -3 to 3
Outputs:
- block_out: bfloat16 [128, 4, 128, 320], P('dp', 'rows')
All inputs are finite; a program needn't handle non-finite values.
Results may differ from a plain program's by a relative error of at most 0.0045.
Values may be sent and summed in bfloat16 or wider, within the bound.
A program may use at most 192 MiB of HBM per device.

v0:
```python
from functools import partial
import jax
import jax.numpy as jnp
from jax import lax
from jax.sharding import PartitionSpec as P


def padded_2(array, sides, width):
    for axis, dim in sides:
        devices, length = (lax.axis_size(axis), array.shape[dim])
        up = [(i, (i + 1) % devices) for i in range(devices - 1)]
        down = [(j, i) for i, j in up]
        last = lax.slice_in_dim(array, length - width, length, axis=dim)
        first = lax.slice_in_dim(array, 0, width, axis=dim)
        before = lax.ppermute(last, axis, up)
        after = lax.ppermute(first, axis, down)
        array = jnp.concatenate([before, array, after], axis=dim)
    return array


def norm_silu(values, group_mean, group_rstd, gain_vec, shift_vec):
    height, columns, channels = values.shape
    groups = group_mean.shape[-1]
    grouped = values.reshape(height, columns, groups, channels // groups)
    scaled = (grouped - group_mean[0][:, None]) * group_rstd[0][:, None]
    return jax.nn.silu(scaled.reshape(height, columns, channels) * gain_vec + shift_vec)


def padded_rows(activation):
    padded = padded_2(activation, (("rows", 0),), 1)
    return jnp.pad(padded, ((0, 0), (1, 1), (0, 0)))


def window_at(padded, position, height, columns, first_channel, depth):
    tap_row = position // 3
    tap_col = position % 3
    window = padded[
        tap_row : tap_row + height,
        tap_col : tap_col + columns,
        first_channel : first_channel + depth,
    ]
    return window.reshape(height * columns, depth)


def convolve_blocks(activation, kernel, blocks):
    height, columns, channels = activation.shape
    padded = padded_rows(activation)
    accumulated = jnp.zeros((height * columns, channels), jnp.float32)
    for number in range(blocks):
        gathered = lax.all_gather(kernel[number], "dp", axis=1, tiled=True)
        depth = gathered.shape[1] // channels
        weights = gathered.reshape(9 * depth, channels)
        windows = jnp.concatenate(
            [
                window_at(padded, position, height, columns, number * depth, depth)
                for position in range(9)
            ],
            axis=1,
        )
        accumulated = accumulated + jnp.dot(windows, weights, preferred_element_type=jnp.float32)
    return accumulated.reshape(height, columns, channels)


def shards(
    latents,
    mean_one,
    rstd_one,
    gain_one,
    shift_one,
    kernel_one,
    bias_one,
    embed_bias,
    mean_two,
    rstd_two,
    gain_two,
    shift_two,
    kernel_two,
    bias_two,
):
    blocks = kernel_one.shape[0]
    sample = latents[0].astype(jnp.float32)
    first_act = norm_silu(sample, mean_one, rstd_one, gain_one, shift_one).astype(jnp.bfloat16)
    conv_one = partial(convolve_blocks, kernel=kernel_one, blocks=blocks)
    conv_two = partial(convolve_blocks, kernel=kernel_two, blocks=blocks)
    hidden = conv_one(first_act) + bias_one + embed_bias[0]
    second_act = norm_silu(hidden, mean_two, rstd_two, gain_two, shift_two).astype(jnp.bfloat16)
    result = conv_two(second_act) + bias_two + sample
    return result.astype(jnp.bfloat16)[None]


def solution(mesh):
    placed = (
        P("dp", "rows", None, None),
        P("dp", None),
        P("dp", None),
        P(),
        P(),
        P(None, None, "dp"),
        P(),
        P("dp", None),
        P("dp", None),
        P("dp", None),
        P(),
        P(),
        P(None, None, "dp"),
        P(),
    )
    return jax.shard_map(
        shards, mesh=mesh, in_specs=placed, out_specs=P("dp", "rows", None, None), check_vma=False
    )
```

profile of v0, /device:TPU:5, one launch (start us, length us, event | category | flops | bytes accessed | tf_op | source)
XLA Modules:
  0.0 1813.6 jit_solution(14008691890563570396)
XLA Ops:
  0.8 0.7 sub.31
  1.7 1.2 fusion.16
  3.5 1.3 collective-permute-start
  4.8 5.5 collective-permute-start.1
  10.3 0.9 fusion.30
  11.4 206.2 %all-gather = bf16[1,9,25600]{1,0,2:T(2,128)(2,1)} all-gather(bf16[1,9,200]{1,0,2:T(2,128)(2,1)S(1)} %copy.181), channel_id=2, replica_groups=mesh['dp'=128,'rows'=2] {'dp'}, dimensions={2}, use_global_device_ids=true | all-gather | bytes 464400 | tf_op jit(solution)/shard_map/all_gather | solution.py:50
  217.8 197.2 %all-gather.1 = bf16[1,9,25600]{1,0,2:T(2,128)(2,1)} all-gather(bf16[1,9,200]{1,0,2:T(2,128)(2,1)S(1)} %copy.182), channel_id=3, replica_groups=mesh['dp'=128,'rows'=2] {'dp'}, dimensions={2}, use_global_device_ids=true | all-gather | bytes 464400 | tf_op jit(solution)/shard_map/all_gather | solution.py:50
  415.1 198.3 %all-gather.2 = bf16[1,9,25600]{1,0,2:T(2,128)(2,1)} all-gather(bf16[1,9,200]{1,0,2:T(2,128)(2,1)S(1)} %copy.183), channel_id=4, replica_groups=mesh['dp'=128,'rows'=2] {'dp'}, dimensions={2}, use_global_device_ids=true | all-gather | bytes 464400 | tf_op jit(solution)/shard_map/all_gather | solution.py:50
  613.5 197.2 %all-gather.3 = bf16[1,9,25600]{1,0,2:T(2,128)(2,1)} all-gather(bf16[1,9,200]{1,0,2:T(2,128)(2,1)S(1)} %copy.184), channel_id=5, replica_groups=mesh['dp'=128,'rows'=2] {'dp'}, dimensions={2}, use_global_device_ids=true | all-gather | bytes 464400 | tf_op jit(solution)/shard_map/all_gather | solution.py:50
  810.9 198.3 %all-gather.4 = bf16[1,9,25600]{1,0,2:T(2,128)(2,1)} all-gather(bf16[1,9,200]{1,0,2:T(2,128)(2,1)S(1)} %copy.185), channel_id=6, replica_groups=mesh['dp'=128,'rows'=2] {'dp'}, dimensions={2}, use_global_device_ids=true | all-gather | bytes 464400 | tf_op jit(solution)/shard_map/all_gather | solution.py:50
  1009.3 197.2 %all-gather.5 = bf16[1,9,25600]{1,0,2:T(2,128)(2,1)} all-gather(bf16[1,9,200]{1,0,2:T(2,128)(2,1)S(1)} %copy.186), channel_id=7, replica_groups=mesh['dp'=128,'rows'=2] {'dp'}, dimensions={2}, use_global_device_ids=true | all-gather | bytes 464400 | tf_op jit(solution)/shard_map/all_gather | solution.py:50
  1206.7 198.4 %all-gather.6 = bf16[1,9,25600]{1,0,2:T(2,128)(2,1)} all-gather(bf16[1,9,200]{1,0,2:T(2,128)(2,1)S(1)} %copy.187), channel_id=8, replica_groups=mesh['dp'=128,'rows'=2] {'dp'}, dimensions={2}, use_global_device_ids=true | all-gather | bytes 464400 | tf_op jit(solution)/shard_map/all_gather | solution.py:50
  1405.1 23.7 %copy.101 = bf16[1,9,25600]{2,1,0:T(8,128)(2,1)S(1)} copy(bf16[1,9,25600]{1,0,2:T(2,128)(2,1)} %all-gather) | data formatting | bytes 921600 | tf_op jit(solution)/shard_map/all_gather | solution.py:50
  1429.3 23.7 %copy.112 = bf16[1,9,25600]{2,1,0:T(8,128)(2,1)S(1)} copy(bf16[1,9,25600]{1,0,2:T(2,128)(2,1)} %all-gather.1) | data formatting | bytes 921600 | tf_op jit(solution)/shard_map/all_gather | solution.py:50
  1453.5 23.7 %copy.123 = bf16[1,9,25600]{2,1,0:T(8,128)(2,1)S(1)} copy(bf16[1,9,25600]{1,0,2:T(2,128)(2,1)} %all-gather.2) | data formatting | bytes 921600 | tf_op jit(solution)/shard_map/all_gather | solution.py:50
  1477.6 23.7 %copy.134 = bf16[1,9,25600]{2,1,0:T(8,128)(2,1)S(1)} copy(bf16[1,9,25600]{1,0,2:T(2,128)(2,1)} %all-gather.3) | data formatting | bytes 921600 | tf_op jit(solution)/shard_map/all_gather | solution.py:50
  1508.1 1.3 collective-permute-start.2
  1509.4 5.5 collective-permute-start.3
  1514.9 197.9 %all-gather.7 = bf16[1,9,25600]{1,0,2:T(2,128)(2,1)} all-gather(bf16[1,9,200]{1,0,2:T(2,128)(2,1)S(1)} %copy.188), channel_id=9, replica_groups=mesh['dp'=128,'rows'=2] {'dp'}, dimensions={2}, use_global_device_ids=true | all-gather | bytes 464400 | tf_op jit(solution)/shard_map/all_gather | solution.py:50
  1712.9 23.7 %copy.146 = bf16[1,9,25600]{2,1,0:T(8,128)(2,1)S(1)} copy(bf16[1,9,25600]{1,0,2:T(2,128)(2,1)} %all-gather.4) | data formatting | bytes 921600 | tf_op jit(solution)/shard_map/all_gather | solution.py:50
  1737.0 23.7 %copy.157 = bf16[1,9,25600]{2,1,0:T(8,128)(2,1)S(1)} copy(bf16[1,9,25600]{1,0,2:T(2,128)(2,1)} %all-gather.5) | data formatting | bytes 921600 | tf_op jit(solution)/shard_map/all_gather | solution.py:50
  1761.2 23.7 %copy.168 = bf16[1,9,25600]{2,1,0:T(8,128)(2,1)S(1)} copy(bf16[1,9,25600]{1,0,2:T(2,128)(2,1)} %all-gather.6) | data formatting | bytes 921600 | tf_op jit(solution)/shard_map/all_gather | solution.py:50
  1785.4 23.7 %copy.179 = bf16[1,9,25600]{2,1,0:T(8,128)(2,1)S(1)} copy(bf16[1,9,25600]{1,0,2:T(2,128)(2,1)} %all-gather.7) | data formatting | bytes 921600 | tf_op jit(solution)/shard_map/all_gather | solution.py:50
  1812.9 0.8 fusion.17
  (141 shorter events, 15.4 us)
Async XLA Ops:
  3.5 1500.7 %collective-permute-start = (bf16[1,128,320]{1,2,0:T(8,128)(2,1)}, bf16[1,128,320]{1,2,0:T(8,128)(2,1)S(1)}, u32[]{:S(2)}, u32[]{:S(2)}) collective-permute-start(bf16[1,128,320]{1,2,0:T(8,128)(2,1)} %get-tuple-element.79), channel_id=1, source_target_pairs={{0,1},{2,3},{4,5},{6,7},{8,9},{10,11},{12,13},{14,15},{16,17},{18,... | collective-permute-start | bytes 245768 | tf_op jit(solution)/shard_map/ppermute | solution.py:15
  4.8 1499.4 %collective-permute-start.1 = (bf16[1,128,320]{1,2,0:T(8,128)(2,1)S(1)}, bf16[1,128,320]{1,2,0:T(8,128)(2,1)S(1)}, u32[]{:S(2)}, u32[]{:S(2)}) collective-permute-start(bf16[1,128,320]{1,2,0:T(8,128)(2,1)S(1)} %get-tuple-element.80), channel_id=1, source_target_pairs={{1,0},{3,2},{5,4},{7,6},{9,8},{11,10},{13,12},{15,14},{17,16},{19,... | collective-permute-start | bytes 245768 | tf_op jit(solution)/shard_map/ppermute | solution.py:16
  613.5 197.2 %copy-start.1 = (bf16[4,9,200]{2,0,1:T(4,128)(2,1)S(1)}, bf16[4,9,200]{2,0,1:T(4,128)(2,1)}, u32[]{:S(2)}) copy-start(bf16[4,9,200]{2,0,1:T(4,128)(2,1)} %param.26) | copy-start | bytes 43204
  1501.3 0.7 copy-start.8
  1501.3 1.4 copy-start.9
  1506.2 0.9 copy-start.2
  1506.2 0.9 copy-start.3
  1506.2 0.9 copy-start.4
  1506.2 0.9 copy-start.5
  1506.3 0.9 copy-start.6
  1508.1 301.4 %collective-permute-start.2 = (bf16[1,128,320]{1,2,0:T(8,128)(2,1)}, bf16[1,128,320]{1,2,0:T(8,128)(2,1)S(1)}, u32[]{:S(2)}, u32[]{:S(2)}) collective-permute-start(bf16[1,128,320]{1,2,0:T(8,128)(2,1)} %get-tuple-element.73), channel_id=1, source_target_pairs={{0,1},{2,3},{4,5},{6,7},{8,9},{10,11},{12,13},{14,15},{16,17},{18,... | collective-permute-start | bytes 245768 | tf_op jit(solution)/shard_map/ppermute | solution.py:15
  1509.4 300.1 %collective-permute-start.3 = (bf16[1,128,320]{1,2,0:T(8,128)(2,1)S(1)}, bf16[1,128,320]{1,2,0:T(8,128)(2,1)S(1)}, u32[]{:S(2)}, u32[]{:S(2)}) collective-permute-start(bf16[1,128,320]{1,2,0:T(8,128)(2,1)S(1)} %get-tuple-element.74), channel_id=1, source_target_pairs={{1,0},{3,2},{5,4},{7,6},{9,8},{11,10},{13,12},{15,14},{17,16},{19,... | collective-permute-start | bytes 245768 | tf_op jit(solution)/shard_map/ppermute | solution.py:16
  1811.9 0.9 copy-start
  1811.9 0.9 copy-start.7
where the time goes:
time: 1820 us; the launch traced here: 1810 us
  blocking collectives  1590 us (87%)
  local copies, waits for them, and re-layouts  201 us (11%)
    all_gather x8, blocking collectives, convolve_blocks(): gathered = lax.all_gather(kernel[number], 'dp', axis=1, tiled=True)  1590 us
    all_gather x8, local copies, waits for them, and re-layouts, convolve_blocks(): gathered = lax.all_gather(kernel[number], 'dp', axis=1, tiled=True)  189 us
  transfers between devices with their start and end apart: 4, of which 0 were waited for; matrix products, arithmetic and copies ran while one was open for 11% of the time, Pallas kernels for 0%

commit v1 on v0

--- a/solution.py
+++ b/solution.py
@@ -47,7 +47,9 @@
     padded = padded_rows(activation)
     accumulated = jnp.zeros((height * columns, channels), jnp.float32)
     for number in range(blocks):
-        gathered = lax.all_gather(kernel[number], "dp", axis=1, tiled=True)
+        gathered = jnp.concatenate(
+            lax.all_to_all(jnp.stack([kernel[number]] * lax.axis_size("dp")), "dp", 0, 0), axis=1
+        )
         depth = gathered.shape[1] // channels
         weights = gathered.reshape(9 * depth, channels)
         windows = jnp.concatenate(

time: 1820 us -> 266 us (0.15)
  the two profiles are of different devices: /device:TPU:5 before, /device:TPU:6 now
where the time goes in v1:
time: 266 us; the launch traced here: 262 us
  waiting for transfers between devices  92.1 us (35%)
  starting transfers between devices  90.8 us (34%)
  local copies, waits for them, and re-layouts  68.2 us (26%)
  other arithmetic  4.7 us (2%)
  matrix products  4.23 us (2%)
    all_to_all x8, waiting for transfers between devices, convolve_blocks(): lax.all_to_all(jnp.stack([kernel[number]] * lax.axis_size('dp')), 'dp', 0...  92 us
    all_to_all x8, starting transfers between devices, convolve_blocks(): lax.all_to_all(jnp.stack([kernel[number]] * lax.axis_size('dp')), 'dp', 0...  75.5 us
    unnamed x124, local copies, waits for them, and re-layouts  51.4 us
    ppermute x2, starting transfers between devices, padded_2(): after = lax.ppermute(first, axis, down)  12.7 us
    another operation x8, local copies, waits for them, and re-layouts, convolve_blocks(): weights = gathered.reshape(9 * depth, channels)  10.2 us
  transfers between devices with their start and end apart: 12, of which 6 were waited for; matrix products, arithmetic and copies ran while one was open for 26% of the time, Pallas kernels for 0%

profile of v1, /device:TPU:6, one launch (start us, length us, event | category | flops | bytes accessed | tf_op | source)
XLA Modules:
  0.0 261.7 jit_solution(3483564723507718437)
XLA Ops:
  4.2 6.1 %collective-permute-start.1 = (bf16[1,128,320]{1,2,0:T(8,128)(2,1)S(1)}, bf16[1,128,320]{1,2,0:T(8,128)(2,1)S(1)}, u32[]{:S(2)}, u32[]{:S(2)}) collective-permute-start(bf16[1,128,320]{1,2,0:T(8,128)(2,1)S(1)} %get-tuple-element.80), channel_id=1, source_target_pairs={{1,0},{3,2},{5,4},{7,6},{9,8},{11,10},{13,12},{15,14},{17,16},{19,... | collective-permute-start | bytes 245768 | tf_op jit(solution)/shard_map/ppermute | solution.py:16
  11.3 2.7 %reshape.381 = bf16[128,2,900]{2,1,0:T(2,128)(2,1)} reshape(bf16[128,9,200]{2,1,0:T(8,128)(2,1)S(1)} %stack.24) | data formatting | bytes 921600
  14.0 14.4 %all-to-all-start = ((bf16[128,2,900]{2,1,0:T(2,128)(2,1)}), bf16[128,2,900]{2,1,0:T(2,128)(2,1)S(1)}, u32[]{:S(2)}, u32[]{:S(2)}) async-start(bf16[128,2,900]{2,1,0:T(2,128)(2,1)} %reshape.381), calls=%async_computation | async-start | bytes 1048576 | tf_op jit(solution)/shard_map/all_to_all | solution.py:51
  31.4 2.7 %reshape.385 = bf16[128,2,900]{2,1,0:T(2,128)(2,1)} reshape(bf16[128,9,200]{2,1,0:T(8,128)(2,1)S(1)} %stack.26) | data formatting | bytes 921600
  34.2 2.7 %reshape.387 = bf16[128,2,900]{2,1,0:T(2,128)(2,1)} reshape(bf16[128,9,200]{2,1,0:T(8,128)(2,1)S(1)} %stack.27) | data formatting | bytes 921600
  37.4 2.7 %reshape.389 = bf16[128,2,900]{2,1,0:T(2,128)(2,1)} reshape(bf16[128,9,200]{2,1,0:T(8,128)(2,1)S(1)} %stack.28) | data formatting | bytes 921600
  40.2 2.7 %reshape.391 = bf16[128,2,900]{2,1,0:T(2,128)(2,1)} reshape(bf16[128,9,200]{2,1,0:T(8,128)(2,1)S(1)} %stack.29) | data formatting | bytes 921600
  45.7 3.2 %reshape.395 = bf16[128,2,900]{2,1,0:T(2,128)(2,1)} reshape(bf16[128,9,200]{2,1,0:T(8,128)(2,1)S(1)} %stack.31) | data formatting | bytes 921600
  50.9 12.4 %all-to-all-start.1 = ((bf16[128,2,900]{2,1,0:T(2,128)(2,1)}), bf16[128,2,900]{2,1,0:T(2,128)(2,1)S(1)}, u32[]{:S(2)}, u32[]{:S(2)}) async-start(bf16[128,2,900]{2,1,0:T(2,128)(2,1)} %reshape.383), calls=%async_computation.1 | async-start | bytes 1048576 | tf_op jit(solution)/shard_map/all_to_all | solution.py:51
  63.4 19.2 %all-to-all-done.1 = bf16[128,2,900]{2,1,0:T(2,128)(2,1)S(1)} async-done(((bf16[128,2,900]{2,1,0:T(2,128)(2,1)}), bf16[128,2,900]{2,1,0:T(2,128)(2,1)S(1)}, u32[]{:S(2)}, u32[]{:S(2)}) %all-to-all-start.1) | async-done | bytes 460832 | tf_op jit(solution)/shard_map/all_to_all | solution.py:51
  82.7 6.8 %all-to-all-start.2 = ((bf16[128,2,900]{2,1,0:T(2,128)(2,1)}), bf16[128,2,900]{2,1,0:T(2,128)(2,1)S(1)}, u32[]{:S(2)}, u32[]{:S(2)}) async-start(bf16[128,2,900]{2,1,0:T(2,128)(2,1)} %reshape.385), calls=%async_computation.2 | async-start | bytes 1048576 | tf_op jit(solution)/shard_map/all_to_all | solution.py:51
  92.6 16.2 %all-to-all-done.2 = bf16[128,2,900]{2,1,0:T(2,128)(2,1)S(1)} async-done(((bf16[128,2,900]{2,1,0:T(2,128)(2,1)}), bf16[128,2,900]{2,1,0:T(2,128)(2,1)S(1)}, u32[]{:S(2)}, u32[]{:S(2)}) %all-to-all-start.2) | async-done | bytes 460832 | tf_op jit(solution)/shard_map/all_to_all | solution.py:51
  108.8 7.9 %all-to-all-start.3 = ((bf16[128,2,900]{2,1,0:T(2,128)(2,1)}), bf16[128,2,900]{2,1,0:T(2,128)(2,1)}, u32[]{:S(2)}, u32[]{:S(2)}) async-start(bf16[128,2,900]{2,1,0:T(2,128)(2,1)} %reshape.387), calls=%async_computation.3 | async-start | bytes 1048576 | tf_op jit(solution)/shard_map/all_to_all | solution.py:51
  117.9 17.7 %all-to-all-done.3 = bf16[128,2,900]{2,1,0:T(2,128)(2,1)} async-done(((bf16[128,2,900]{2,1,0:T(2,128)(2,1)}), bf16[128,2,900]{2,1,0:T(2,128)(2,1)}, u32[]{:S(2)}, u32[]{:S(2)}) %all-to-all-start.3) | async-done | bytes 460832 | tf_op jit(solution)/shard_map/all_to_all | solution.py:51
  135.6 6.8 %all-to-all-start.4 = ((bf16[128,2,900]{2,1,0:T(2,128)(2,1)}), bf16[128,2,900]{2,1,0:T(2,128)(2,1)S(1)}, u32[]{:S(2)}, u32[]{:S(2)}) async-start(bf16[128,2,900]{2,1,0:T(2,128)(2,1)} %reshape.389), calls=%async_computation.4 | async-start | bytes 1048576 | tf_op jit(solution)/shard_map/all_to_all | solution.py:51
  142.5 19.2 %all-to-all-done.4 = bf16[128,2,900]{2,1,0:T(2,128)(2,1)S(1)} async-done(((bf16[128,2,900]{2,1,0:T(2,128)(2,1)}), bf16[128,2,900]{2,1,0:T(2,128)(2,1)S(1)}, u32[]{:S(2)}, u32[]{:S(2)}) %all-to-all-start.4) | async-done | bytes 460832 | tf_op jit(solution)/shard_map/all_to_all | solution.py:51
  161.8 6.8 %all-to-all-start.5 = ((bf16[128,2,900]{2,1,0:T(2,128)(2,1)}), bf16[128,2,900]{2,1,0:T(2,128)(2,1)S(1)}, u32[]{:S(2)}, u32[]{:S(2)}) async-start(bf16[128,2,900]{2,1,0:T(2,128)(2,1)} %reshape.391), calls=%async_computation.5 | async-start | bytes 1048576 | tf_op jit(solution)/shard_map/all_to_all | solution.py:51
  168.7 19.2 %all-to-all-done.5 = bf16[128,2,900]{2,1,0:T(2,128)(2,1)S(1)} async-done(((bf16[128,2,900]{2,1,0:T(2,128)(2,1)}), bf16[128,2,900]{2,1,0:T(2,128)(2,1)S(1)}, u32[]{:S(2)}, u32[]{:S(2)}) %all-to-all-start.5) | async-done | bytes 460832 | tf_op jit(solution)/shard_map/all_to_all | solution.py:51
  187.9 7.9 %all-to-all-start.6 = ((bf16[128,2,900]{2,1,0:T(2,128)(2,1)}), bf16[128,2,900]{2,1,0:T(2,128)(2,1)}, u32[]{:S(2)}, u32[]{:S(2)}) async-start(bf16[128,2,900]{2,1,0:T(2,128)(2,1)} %reshape.393), calls=%async_computation.6 | async-start | bytes 1048576 | tf_op jit(solution)/shard_map/all_to_all | solution.py:51
  207.1 3.7 %reshape.388 = bf16[128,9,200]{2,1,0:T(8,128)(2,1)S(1)} reshape(bf16[128,2,900]{2,1,0:T(2,128)(2,1)} %all-to-all-done.3) | data formatting | bytes 921600
  214.7 12.4 %all-to-all-start.7 = ((bf16[128,2,900]{2,1,0:T(2,128)(2,1)}), bf16[128,2,900]{2,1,0:T(2,128)(2,1)}, u32[]{:S(2)}, u32[]{:S(2)}) async-start(bf16[128,2,900]{2,1,0:T(2,128)(2,1)} %reshape.395), calls=%async_computation.7 | async-start | bytes 1048576 | tf_op jit(solution)/shard_map/all_to_all | solution.py:51
  231.1 6.7 %collective-permute-start.3 = (bf16[1,128,320]{1,2,0:T(8,128)(2,1)}, bf16[1,128,320]{1,2,0:T(8,128)(2,1)}, u32[]{:S(2)}, u32[]{:S(2)}) collective-permute-start(bf16[1,128,320]{1,2,0:T(8,128)(2,1)} %get-tuple-element.74), channel_id=1, source_target_pairs={{1,0},{3,2},{5,4},{7,6},{9,8},{11,10},{13,12},{15,14},{17,16},{19,... | collective-permute-start | bytes 245768 | tf_op jit(solution)/shard_map/ppermute | solution.py:16
  245.3 3.7 %reshape.394 = bf16[128,9,200]{2,1,0:T(8,128)(2,1)S(1)} reshape(bf16[128,2,900]{2,1,0:T(2,128)(2,1)} %all-to-all-done.6) | data formatting | bytes 921600
  250.6 3.5 %reshape.396 = bf16[128,9,200]{2,1,0:T(8,128)(2,1)S(1)} reshape(bf16[128,2,900]{2,1,0:T(2,128)(2,1)} %all-to-all-done.7) | data formatting | bytes 921600
  (191 shorter events, 52.6 us)
Async XLA Ops:
  2.9 46.1 %collective-permute-start = (bf16[1,128,320]{1,2,0:T(8,128)(2,1)S(1)}, bf16[1,128,320]{1,2,0:T(8,128)(2,1)S(1)}, u32[]{:S(2)}, u32[]{:S(2)}) collective-permute-start(bf16[1,128,320]{1,2,0:T(8,128)(2,1)S(1)} %get-tuple-element.79), channel_id=1, source_target_pairs={{0,1},{2,3},{4,5},{6,7},{8,9},{10,11},{12,13},{14,15},{16,17},{18,... | collective-permute-start | bytes 245768 | tf_op jit(solution)/shard_map/ppermute | solution.py:15
  4.2 44.8 %collective-permute-start.1 = (bf16[1,128,320]{1,2,0:T(8,128)(2,1)S(1)}, bf16[1,128,320]{1,2,0:T(8,128)(2,1)S(1)}, u32[]{:S(2)}, u32[]{:S(2)}) collective-permute-start(bf16[1,128,320]{1,2,0:T(8,128)(2,1)S(1)} %get-tuple-element.80), channel_id=1, source_target_pairs={{1,0},{3,2},{5,4},{7,6},{9,8},{11,10},{13,12},{15,14},{17,16},{19,... | collective-permute-start | bytes 245768 | tf_op jit(solution)/shard_map/ppermute | solution.py:16
  11.3 17.2 %copy-start.13 = (bf16[4,9,200]{2,0,1:T(4,128)(2,1)S(1)}, bf16[4,9,200]{2,0,1:T(4,128)(2,1)}, u32[]{:S(2)}) copy-start(bf16[4,9,200]{2,0,1:T(4,128)(2,1)} %param.26) | copy-start | bytes 43204
  14.0 36.9 %all-to-all-start = ((bf16[128,2,900]{2,1,0:T(2,128)(2,1)}), bf16[128,2,900]{2,1,0:T(2,128)(2,1)S(1)}, u32[]{:S(2)}, u32[]{:S(2)}) async-start(bf16[128,2,900]{2,1,0:T(2,128)(2,1)} %reshape.381), calls=%async_computation | async-start | bytes 1048576 | tf_op jit(solution)/shard_map/all_to_all | solution.py:51
  34.2 2.7 %copy-start.19 = (f32[1,32]{1,0:T(1,128)S(1)}, f32[1,32]{1,0:T(1,128)}, u32[]{:S(2)}) copy-start(f32[1,32]{1,0:T(1,128)} %param.23) | copy-start | bytes 388
  34.2 2.9 %copy-start.20 = (f32[1,32]{1,0:T(1,128)S(1)}, f32[1,32]{1,0:T(1,128)}, u32[]{:S(2)}) copy-start(f32[1,32]{1,0:T(1,128)} %param.22) | copy-start | bytes 388
  45.7 3.2 %copy-start.18 = (f32[1,320]{1,0:T(1,128)S(1)}, f32[1,320]{1,0:T(1,128)}, u32[]{:S(2)}) copy-start(f32[1,320]{1,0:T(1,128)} %param.21) | copy-start | bytes 3844
  50.9 31.7 %all-to-all-start.1 = ((bf16[128,2,900]{2,1,0:T(2,128)(2,1)}), bf16[128,2,900]{2,1,0:T(2,128)(2,1)S(1)}, u32[]{:S(2)}, u32[]{:S(2)}) async-start(bf16[128,2,900]{2,1,0:T(2,128)(2,1)} %reshape.383), calls=%async_computation.1 | async-start | bytes 1048576 | tf_op jit(solution)/shard_map/all_to_all | solution.py:51
  63.4 19.2 %copy-start.11 = (bf16[256,720]{0,1:T(8,128)(2,1)}, bf16[256,720]{0,1:T(8,128)(2,1)S(1)}, u32[]{:S(2)}) copy-start(bf16[256,720]{0,1:T(8,128)(2,1)S(1)} %constant_dynamic-update-slice_fusion.9) | copy-start | bytes 1105924
  82.7 26.1 %all-to-all-start.2 = ((bf16[128,2,900]{2,1,0:T(2,128)(2,1)}), bf16[128,2,900]{2,1,0:T(2,128)(2,1)S(1)}, u32[]{:S(2)}, u32[]{:S(2)}) async-start(bf16[128,2,900]{2,1,0:T(2,128)(2,1)} %reshape.385), calls=%async_computation.2 | async-start | bytes 1048576 | tf_op jit(solution)/shard_map/all_to_all | solution.py:51
  108.8 26.8 %copy-start = (bf16[128,2,900]{2,1,0:T(2,128)(2,1)}, bf16[128,2,900]{2,1,0:T(2,128)(2,1)S(1)}, u32[]{:S(2)}) copy-start(bf16[128,2,900]{2,1,0:T(2,128)(2,1)S(1)} %all-to-all-done.2) | copy-start | bytes 1382404
  108.8 26.8 %all-to-all-start.3 = ((bf16[128,2,900]{2,1,0:T(2,128)(2,1)}), bf16[128,2,900]{2,1,0:T(2,128)(2,1)}, u32[]{:S(2)}, u32[]{:S(2)}) async-start(bf16[128,2,900]{2,1,0:T(2,128)(2,1)} %reshape.387), calls=%async_computation.3 | async-start | bytes 1048576 | tf_op jit(solution)/shard_map/all_to_all | solution.py:51
  135.6 26.1 %all-to-all-start.4 = ((bf16[128,2,900]{2,1,0:T(2,128)(2,1)}), bf16[128,2,900]{2,1,0:T(2,128)(2,1)S(1)}, u32[]{:S(2)}, u32[]{:S(2)}) async-start(bf16[128,2,900]{2,1,0:T(2,128)(2,1)} %reshape.389), calls=%async_computation.4 | async-start | bytes 1048576 | tf_op jit(solution)/shard_map/all_to_all | solution.py:51
  142.5 45.3 %copy-start.7 = (bf16[256,720]{0,1:T(8,128)(2,1)}, bf16[256,720]{0,1:T(8,128)(2,1)S(1)}, u32[]{:S(2)}) copy-start(bf16[256,720]{0,1:T(8,128)(2,1)S(1)} %constant_dynamic-update-slice_fusion.18) | copy-start | bytes 1105924
  161.8 26.1 %copy-start.2 = (bf16[128,2,900]{2,1,0:T(2,128)(2,1)}, bf16[128,2,900]{2,1,0:T(2,128)(2,1)S(1)}, u32[]{:S(2)}) copy-start(bf16[128,2,900]{2,1,0:T(2,128)(2,1)S(1)} %all-to-all-done.4) | copy-start | bytes 1382404
  161.8 26.1 %all-to-all-start.5 = ((bf16[128,2,900]{2,1,0:T(2,128)(2,1)}), bf16[128,2,900]{2,1,0:T(2,128)(2,1)S(1)}, u32[]{:S(2)}, u32[]{:S(2)}) async-start(bf16[128,2,900]{2,1,0:T(2,128)(2,1)} %reshape.391), calls=%async_computation.5 | async-start | bytes 1048576 | tf_op jit(solution)/shard_map/all_to_all | solution.py:51
  187.9 7.9 %copy-start.4 = (bf16[128,2,900]{2,1,0:T(2,128)(2,1)}, bf16[128,2,900]{2,1,0:T(2,128)(2,1)S(1)}, u32[]{:S(2)}) copy-start(bf16[128,2,900]{2,1,0:T(2,128)(2,1)S(1)} %all-to-all-done.5) | copy-start | bytes 1382404
  187.9 26.8 %all-to-all-start.6 = ((bf16[128,2,900]{2,1,0:T(2,128)(2,1)}), bf16[128,2,900]{2,1,0:T(2,128)(2,1)}, u32[]{:S(2)}, u32[]{:S(2)}) async-start(bf16[128,2,900]{2,1,0:T(2,128)(2,1)} %reshape.393), calls=%async_computation.6 | async-start | bytes 1048576 | tf_op jit(solution)/shard_map/all_to_all | solution.py:51
  195.8 2.3 copy-start.9
  213.8 13.3 %copy-start.8 = (bf16[256,720]{0,1:T(8,128)(2,1)S(1)}, bf16[256,720]{0,1:T(8,128)(2,1)}, u32[]{:S(2)}) copy-start(bf16[256,720]{0,1:T(8,128)(2,1)} %copy-done.7) | copy-start | bytes 1105924
  214.7 35.8 %all-to-all-start.7 = ((bf16[128,2,900]{2,1,0:T(2,128)(2,1)}), bf16[128,2,900]{2,1,0:T(2,128)(2,1)}, u32[]{:S(2)}, u32[]{:S(2)}) async-start(bf16[128,2,900]{2,1,0:T(2,128)(2,1)} %reshape.395), calls=%async_computation.7 | async-start | bytes 1048576 | tf_op jit(solution)/shard_map/all_to_all | solution.py:51
  228.1 9.7 %copy-start.3 = (bf16[128,2,900]{2,1,0:T(2,128)(2,1)S(1)}, bf16[128,2,900]{2,1,0:T(2,128)(2,1)}, u32[]{:S(2)}) copy-start(bf16[128,2,900]{2,1,0:T(2,128)(2,1)} %copy-done.2) | copy-start | bytes 1382404
  229.8 25.7 %collective-permute-start.2 = (bf16[1,128,320]{1,2,0:T(8,128)(2,1)}, bf16[1,128,320]{1,2,0:T(8,128)(2,1)S(1)}, u32[]{:S(2)}, u32[]{:S(2)}) collective-permute-start(bf16[1,128,320]{1,2,0:T(8,128)(2,1)} %get-tuple-element.73), channel_id=1, source_target_pairs={{0,1},{2,3},{4,5},{6,7},{8,9},{10,11},{12,13},{14,15},{16,17},{18,... | collective-permute-start | bytes 245768 | tf_op jit(solution)/shard_map/ppermute | solution.py:15
  231.1 24.4 %collective-permute-start.3 = (bf16[1,128,320]{1,2,0:T(8,128)(2,1)}, bf16[1,128,320]{1,2,0:T(8,128)(2,1)}, u32[]{:S(2)}, u32[]{:S(2)}) collective-permute-start(bf16[1,128,320]{1,2,0:T(8,128)(2,1)} %get-tuple-element.74), channel_id=1, source_target_pairs={{1,0},{3,2},{5,4},{7,6},{9,8},{11,10},{13,12},{15,14},{17,16},{19,... | collective-permute-start | bytes 245768 | tf_op jit(solution)/shard_map/ppermute | solution.py:16
  (9 other events, 9.4 us)
